TPU v7x, 256 devices: a whole 4x4x8 slice. The times are simulated.
256 devices in a mesh: replica: 8 (over y_lo, x), fsdp: 32 (over y_hi, z, core).
Axes of the slice: x: 4, y: 4 (y_hi: 2, y_lo: 2; y = y_hi * 2 + y_lo), z: 8, core: 2. Of those that a mesh axis runs over, the one named last changes fastest.
Arguments:
- hidden: bfloat16 [65536, 10240], P(('replica', 'fsdp')), may hold values from -6 to 6
- norm_gain: float32 [10240], replicated, may hold values from 0.5 to 1.5
- local_weight: bfloat16 [8, 10240, 1024], P('replica', 'fsdp'), may hold values from -6 to 6
- global_weight: float32 [10240, 1024], P('fsdp'), may hold values from -6 to 6
- momentum: float32 [10240, 1024], P('fsdp'), may hold values from -4 to 4
Outputs:
- keys: bfloat16 [65536, 1024], P(('replica', 'fsdp'))
- new_global: float32 [10240, 1024], P('fsdp')
- new_momentum: float32 [10240, 1024], P('fsdp')
All inputs are finite; a program needn't handle non-finite values.
Results may differ from a plain program's by a relative error of at most 0.019.
Values may be sent and summed in bfloat16 or wider, within the bound.
A program may use at most 128 MiB of HBM per device.

v0:
```python
import math

import jax
import jax.numpy as jnp
from jax import lax
from jax.sharding import PartitionSpec as P

BLOCK = 128


def normed_rows(block_rows, norm_gain):
    floats = block_rows.astype(jnp.float32)
    inverse = lax.rsqrt(jnp.mean(floats * floats, axis=-1, keepdims=True) + 1e-05)
    return (floats * inverse * norm_gain).astype(jnp.bfloat16)


def shards(hidden, norm_gain, local_weight, global_weight, momentum):
    features = hidden.shape[1]
    factor = 1.0 / math.sqrt(features)
    weight_rows = local_weight[0]
    own_rows, width = weight_rows.shape
    normed = normed_rows(hidden, norm_gain)
    summed = jnp.dot(
        normed,
        lax.all_gather(weight_rows, "fsdp", axis=0, tiled=True),
        preferred_element_type=jnp.float32,
    )
    keys = (summed * factor).astype(jnp.bfloat16)
    replicas = lax.axis_size("replica")
    groups = width // BLOCK
    delta = global_weight - weight_rows.astype(jnp.float32)
    blocks = delta.reshape(own_rows, groups, BLOCK)
    scale = (jnp.max(jnp.abs(blocks), axis=-1) + 1e-06).astype(jnp.bfloat16)
    code = (blocks / scale[..., None].astype(jnp.float32)).astype(jnp.bfloat16)
    all_codes, all_scales = (
        lax.all_gather(code[None], "replica", axis=0, tiled=True),
        lax.all_gather(scale[None], "replica", axis=0, tiled=True),
    )
    decoded = all_codes.astype(jnp.float32) * all_scales[..., None].astype(jnp.float32)
    mean_delta = (jnp.sum(decoded, axis=0) / replicas).reshape(own_rows, width)
    new_momentum = 0.9 * momentum + mean_delta
    new_global = global_weight - 0.7 * (0.9 * new_momentum + mean_delta)
    return (keys, new_global, new_momentum)


def solution(mesh):
    return jax.shard_map(
        shards,
        mesh=mesh,
        in_specs=(
            P(("replica", "fsdp"), None),
            P(),
            P("replica", "fsdp", None),
            P("fsdp", None),
            P("fsdp", None),
        ),
        out_specs=(P(("replica", "fsdp"), None), P("fsdp", None), P("fsdp", None)),
        check_vma=False,
    )
```

profile of v0, /device:TPU:1, one launch (start us, length us, event | category | flops | bytes accessed | tf_op | source)
XLA Modules:
  0.0 262.4 jit_solution(7963123993180068124)
XLA Ops:
  7.2 0.0 all-gather.6.cloned.1.call-start
  7.2 1.7 abs_bitcast_fusion
  8.9 0.3 copy.13
  9.2 0.4 reduce_max.9
  9.6 0.3 copy.12
  9.9 1.2 fusion.15
  11.2 0.0 all-gather.6.cloned.1.call-update
  11.2 0.0 all-gather.8.cloned.1.call-start
  11.2 0.7 all-gather.8.cloned.1.call-update
  11.9 0.1 copy.10
  12.0 24.0 %all-gather.2 = bf16[8,320,8]{1,2,0:T(8,128)(2,1)S(1)} all-gather(bf16[1,320,8]{1,2,0:T(8,128)(2,1)S(1)} %copy.10), channel_id=3, replica_groups=mesh['replica'=8,'fsdp'=32] {'replica'}, dimensions={0}, use_global_device_ids=true | all-gather | bytes 46080 | tf_op jit(solution)/shard_map/all_gather | solution.py:37
  36.0 0.3 copy.11
  36.2 3.7 %fusion.2 = f32[256]{0:T(256)S(1)} fusion(bf16[256,10240]{1,0:T(8,128)(2,1)} %param.5), kind=kLoop, calls=%fused_computation.4 | loop fusion | flops 7864064 | bytes 5243904 | tf_op jit(solution)/shard_map/reduce_sum | solution.py:13
  39.9 40.4 %all-gather.6.cloned.1.call-done = bf16[8,320,8,128]{3,2,1,0:T(8,128)(2,1)} async-done(((bf16[1,320,8,128]{3,2,1,0:T(8,128)(2,1)}), bf16[8,320,8,128]{3,2,1,0:T(8,128)(2,1)}) %all-gather.6.cloned.1.call-update) | async-done | bytes 5242896 | tf_op jit(solution)/shard_map/all_gather | solution.py:36
  80.4 6.2 %multiply_reduce_fusion = f32[320,8,128]{2,1,0:T(8,128)S(1)} fusion(bf16[8,320,8,128]{3,2,1,0:T(8,128)(2,1)} %all-gather.6.cloned.1.call-done, f32[8,320,8]{2,1,0:T(8,128)S(1)} %copy.11), kind=kLoop, calls=%fused_computation.7 | loop fusion | flops 7536640 | bytes 6635520 | tf_op jit(solution)/shard_map/reduce_sum | solution.py:40
  86.5 0.0 copy-start
  86.5 0.0 copy-start.1
  86.6 0.1 broadcast_multiply_fusion
  86.7 1.2 copy-done
  87.9 0.4 copy-done.1
  88.2 0.0 copy-start.2
  88.3 2.1 fusion.14
  90.4 150.8 %all-gather.8.cloned.1.call-done = bf16[1,10240,1024]{2,1,0:T(8,128)(2,1)} async-done(((bf16[1,320,1024]{2,1,0:T(8,128)(2,1)}), bf16[1,10240,1024]{2,1,0:T(8,128)(2,1)}) %all-gather.8.cloned.1.call-update) | async-done | bytes 20971536 | tf_op jit(solution)/shard_map/all_gather | solution.py:25
  241.1 0.0 copy-done.2
  241.1 14.4 %fusion.16 = bf16[256,1024]{1,0:T(8,128)(2,1)} fusion(bf16[1,10240,1024]{2,1,0:T(8,128)(2,1)} %all-gather.8.cloned.1.call-done, bf16[256,10240]{1,0:T(8,128)(2,1)} %param.5, f32[10240]{0:T(1024)S(1)} %copy-done.2, f32[256]{0:T(256)S(1)} %add_rsqrt_fusion), kind=kOutput, calls=%fused_computation.19 | convolution fusion | flops 5379719168 | bytes 26780672 | tf_op jit(solution)/shard_map/dot_general | solution.py:23
  (2 shorter events, 0.0 us)
Async XLA Ops:
  7.2 73.2 %all-gather.6.cloned.1.call-start = ((), (), s32[]{:S(2)}) async-start(), calls=%async_computation | async-start | bytes 5898240 | tf_op jit(solution)/shard_map/all_gather | solution.py:36
  11.2 229.9 %all-gather.8.cloned.1.call-start = ((), (), s32[]{:S(2)}) async-start(), calls=%async_computation.1 | async-start | bytes 21626880 | tf_op jit(solution)/shard_map/all_gather | solution.py:25
  86.5 1.3 copy-start
  86.5 1.7 copy-start.1
  88.2 152.9 %copy-start.2 = (f32[10240]{0:T(1024)S(1)}, f32[10240]{0:T(1024)}, u32[]{:S(2)}) copy-start(f32[10240]{0:T(1024)} %param.6) | copy-start | bytes 122884
Sparse Core Ops, SparseCore 0:
  11.3 69.0 all-gather.5
  83.1 157.9 all-gather.7
where the time goes:
time: 263 us; the launch traced here: 262 us
  waiting for transfers between devices  192 us (73%)
  blocking collectives  24 us (9%)
  other arithmetic  15.4 us (6%)
  matrix products  14.4 us (5%)
  between operations  14.1 us (5%)
    all_gather x1, waiting for transfers between devices, shards(): lax.all_gather(weight_rows, 'fsdp', axis=0, tiled=True)  151 us
    all_gather x1, waiting for transfers between devices, shards(): lax.all_gather(code[None], 'replica', axis=0, tiled=True)  40.4 us
    all_gather x1, blocking collectives, shards(): lax.all_gather(scale[None], 'replica', axis=0, tiled=True)  24 us
    dot_general x1, matrix products, shards(): jnp.dot(normed, lax.all_gather(weight_rows, 'fsdp', axis=0, tiled=True),...  14.4 us
    reduce_sum x1, other arithmetic, shards(): mean_delta = (jnp.sum(decoded, axis=0) / replicas).reshape(own_rows, width)  6.17 us
  transfers between devices with their start and end apart: 2, of which 2 were waited for; matrix products, arithmetic and copies ran while one was open for 5% of the time, Pallas kernels for 0%

commit v1 on v0

v1 whole, which is shorter than its diff:
```python
import functools
import math

import jax
import jax.numpy as jnp
from jax import lax
from jax.experimental import pallas as pl
from jax.experimental.pallas import tpu as pltpu
from jax.sharding import PartitionSpec as P

MESH = pl.DeviceIdType.MESH
BLOCK = 128
F32 = jnp.float32
BF16 = jnp.bfloat16

RING = (
    ("B", 0, 0), ("B", 1, 0), ("B", 0, 1), ("B", 1, 1), ("A", 0, 0), ("A", 1, 0), ("B", 0, 2),
    ("B", 1, 2), ("B", 0, 3), ("A", 0, 1), ("A", 1, 1), ("A", 0, 2), ("A", 1, 2), ("A", 0, 3),
)
N_RING = len(RING)


def kernel(
    ws, hid, wl_in, g_in, m_in, keys_out, ng_out, nm_out,
    H, HP, WB, WX, acc, PS, PR, wl, gl, mo, dec, rsb, ysend, yrecv, mean, ng, nm, inv, KO, KS,
    loc, sib_s, sib_r, rel_s, rel_r, z_s, z_r, yc_s, yc_r, yh_s, yh_r, yp_s, yp_r, x_s, x_r, xg_s, xg_r, yl_s, yl_r,
):
    replica, fsdp = lax.axis_index("replica"), lax.axis_index("fsdp")
    x, ylo = lax.rem(replica, 4), lax.div(replica, 4)
    c, z, r = lax.rem(fsdp, 2), lax.rem(lax.div(fsdp, 2), 8), lax.div(fsdp, 16)
    o = 1 - c

    def at_fsdp(r_, z_, c_):
        return (replica, r_ * 16 + z_ * 2 + c_)

    sib = at_fsdp(r, z, o)
    zdev = (at_fsdp(r, lax.rem(z + 1, 8), c), at_fsdp(r, lax.rem(z + 7, 8), c))
    partner = at_fsdp(1 - r, z, c)
    xdev = [(ylo * 4 + lax.rem(x + j, 4), fsdp) for j in (1, 2, 3)]
    ydev = ((1 - ylo) * 4 + x, fsdp)

    def remote(src, dst, s, rcv, dev):
        return pltpu.make_async_remote_copy(
            src_ref=src, dst_ref=dst, send_sem=s, recv_sem=rcv, device_id=dev, device_id_type=MESH
        )

    l_h = pltpu.make_async_copy(hid, H.at[pl.ds(pl.multiple_of(c * 256, 256), 256)], loc.at[0])
    own_cols = pl.ds(pl.multiple_of(c * 512, 512), 512)
    oth_cols = pl.ds(pl.multiple_of(o * 512, 512), 512)
    own_rows = pl.ds(pl.multiple_of(c * 320, 64), 320)
    l_w = pltpu.make_async_copy(ws.at[:, own_cols], WB.at[z, own_rows], loc.at[1])
    l_wl = pltpu.make_async_copy(wl_in, wl, loc.at[2])
    l_g = pltpu.make_async_copy(g_in, gl, loc.at[3])
    l_m = pltpu.make_async_copy(m_in, mo, loc.at[4])
    l_w.start()
    l_wl.start()
    l_g.start()
    l_h.start()
    l_m.start()

    barrier = pltpu.get_barrier_semaphore()
    everyone = [sib, zdev[0], zdev[1], partner, ydev] + xdev
    for dev in everyone:
        pl.semaphore_signal(barrier, inc=1, device_id=dev, device_id_type=MESH)
    pl.semaphore_wait(barrier, len(everyone))

    w_sib = remote(ws.at[:, oth_cols], WB.at[z, own_rows], sib_s.at[0], sib_r.at[0], sib)
    w_sib.start()

    def hid_group(q):
        g, half = divmod(q, 2)
        out = []
        for zb in range(half * 4, half * 4 + 4):
            col = pl.multiple_of((1 - r) * 5120 + zb * 640, 128)
            out.append(remote(
                hid.at[pl.ds(g * 128, 128), pl.ds(col, 512)],
                HP.at[g, pl.ds(pl.multiple_of(c * 128, 128), 128), pl.ds(zb * 512, 512)],
                yh_s.at[q, zb % 4], yh_r.at[q, zb % 4], partner,
            ))
        return out

    def relay(q):
        g, half = divmod(q, 2)
        part = HP.at[g, pl.ds(pl.multiple_of(c * 128, 128), 128), pl.ds(half * 2048, 2048)]
        return remote(part, part, rel_s.at[q], rel_r.at[q], sib)

    groups = [hid_group(q) for q in range(4)]
    relays = [relay(q) for q in range(4)]

    def chunk_ref(kind, half, slot):
        if kind == "B":
            return WB.at[slot, pl.ds(half * 256, 256)]
        if half == 0:
            return WB.at[slot, pl.ds(512, 128)]
        return WX.at[slot]

    def slot_of(way, dist):
        return lax.rem(z + (8 - dist if way == 0 else dist), 8)

    def ring_copy(way, i):
        kind, half, dist = RING[i]
        part = chunk_ref(kind, half if way == 0 else 1 - half, slot_of(way, dist))
        return remote(part, part, z_s.at[way, i], z_r.at[way, i], zdev[way])

    ring = [[ring_copy(way, i) for i in range(N_RING)] for way in range(2)]

    l_w.wait()
    w_sib.wait_recv()
    for i in range(2):
        for way in range(2):
            ring[way][i].start()
    cross = remote(WB.at[z, pl.ds(512, 128)], WX.at[z], yc_s, yc_r, partner)
    cross.start()
    for cp in groups[0]:
        cp.start()
    h_sib = remote(
        hid, H.at[pl.ds(pl.multiple_of(c * 256, 256), 256)], sib_s.at[1], sib_r.at[1], sib
    )
    h_sib.start()
    for cp in groups[1]:
        cp.start()

    l_wl.wait()
    l_g.wait()

    @pl.loop(0, 20)
    def _(i):
        rows = pl.ds(pl.multiple_of(i * 16, 16), 16)
        for b in range(8):
            cols = pl.ds(b * BLOCK, BLOCK)
            d = gl[rows, cols] - wl[rows, cols].astype(F32)
            s = (jnp.max(jnp.abs(d), axis=-1, keepdims=True) + 1e-06).astype(BF16).astype(F32)
            dec[rows, cols] = (d / s).astype(BF16).astype(F32) * s

    def quarter(q):
        return pl.ds(pl.multiple_of(q * 80, 16), 80)

    scatter = [
        remote(dec.at[quarter(lax.rem(x + j, 4))], rsb.at[j - 1], x_s.at[j - 1], x_r.at[j - 1], xdev[j - 1])
        for j in (1, 2, 3)
    ]
    for cp in scatter:
        cp.start()
    ysum = remote(ysend, yrecv, yl_s, yl_r, ydev)
    spread = [
        remote(mean.at[quarter(x)], mean.at[quarter(x)], xg_s.at[j - 1], xg_r.at[j - 1], xdev[j - 1])
        for j in (1, 2, 3)
    ]
    acc[...] = jnp.zeros_like(acc)

    def mm(h_col, w_ref, depth):
        for n in range(2):
            cols = pl.ds(n * 256, 256)
            acc[:, cols] += jnp.dot(
                H[:, pl.ds(pl.multiple_of(h_col, 128), depth)], w_ref[:, cols], preferred_element_type=F32
            )

    def mm_chunk(kind, half, slot):
        base = slot * 640
        if kind == "B":
            mm(r * 5120 + base + half * 256, chunk_ref(kind, half, slot), 256)
        elif half == 0:
            mm(r * 5120 + base + 512, chunk_ref(kind, half, slot), 128)
        else:
            mm((1 - r) * 5120 + base + 512, chunk_ref(kind, half, slot), 128)

    def mm_arrival(i):
        kind, half, dist = RING[i]
        if kind == "B":
            @pl.loop(0, 2)
            def _(way):
                slot = lax.rem(z + 8 + (2 * way - 1) * (dist + 1), 8)
                h_ = way if half == 0 else 1 - way
                mm(
                    r * 5120 + slot * 640 + h_ * 256,
                    WB.at[slot, pl.ds(pl.multiple_of(h_ * 256, 256), 256)], 256,
                )
        else:
            for way in range(2):
                mm_chunk(kind, half if way == 0 else 1 - half, slot_of(way, dist + 1))

    def mean_squares(part):
        @pl.loop(0, 4)
        def _(i):
            rows = pl.ds(pl.multiple_of(part * 256 + i * 64, 64), 64)

            def body(k, total):
                for s in range(4):
                    v = H[rows, pl.ds(pl.multiple_of(k * 512 + s * 128, 128), 128)].astype(F32)
                    total = total + v * v
                return total

            total = lax.fori_loop(0, 20, body, jnp.zeros((64, 128), F32))
            ms = jnp.sum(total, axis=-1, keepdims=True) * (1.0 / 10240)
            inv[rows, :] = jnp.broadcast_to(lax.rsqrt(ms + 1e-05) * (1.0 / math.sqrt(10240)), (64, 128))

    def partner_sums(g):
        for n in range(2):
            cols = pl.ds(n * 256, 256)

            def body(s, total):
                return total + jnp.dot(
                    HP[g, :, pl.ds(pl.multiple_of(s * 512, 512), 512)],
                    WB[s, pl.ds(0, 512), cols], preferred_element_type=F32,
                )

            PS[g, :, cols] = lax.fori_loop(0, 8, body, jnp.zeros((256, 256), F32)).astype(BF16)

    back = [remote(PS.at[g], PR.at[g], yp_s.at[g], yp_r.at[g], partner) for g in range(2)]

    def take_relay(q):
        for cp in groups[q]:
            cp.wait_recv()
        relays[q].start()
        if q + 2 < 4:
            for cp in groups[q + 2]:
                cp.start()

    for i in range(N_RING):
        for way in range(2):
            ring[way][i].wait_recv()
            if i + 2 < N_RING:
                if i == 2 and way == 0:
                    cross.wait_recv()
                ring[way][i + 2].start()
        if i == 2:
            l_h.wait()
            h_sib.wait_recv()
            take_relay(0)
            for half in range(2):
                mm_chunk("B", half, z)
                mm_chunk("A", half, z)
            for k in range(3):
                mm_arrival(k)
            for cp in scatter:
                cp.wait_recv()
            for k in range(5):
                rows = pl.ds(k * 16, 16)
                own = dec[pl.ds(pl.multiple_of(x * 80 + k * 16, 16), 16), :]
                ysend[rows, :] = (own + rsb[0, rows, :] + rsb[1, rows, :] + rsb[2, rows, :]).astype(BF16)
            ysum.start()
        elif i > 2:
            mm_arrival(i)
        if i == 3:
            mean_squares(0)
        if i == 4:
            mean_squares(1)
        if i == 5:
            ysum.wait_recv()
            for k in range(5):
                rows = pl.ds(k * 16, 16)
                mean[pl.ds(pl.multiple_of(x * 80 + k * 16, 16), 16), :] = (
                    ysend[rows, :].astype(F32) + yrecv[rows, :].astype(F32)
                ) * 0.125
            for cp in spread:
                cp.start()
        if i == 6:
            take_relay(1)
        if i == 8:
            relays[0].wait_recv()
            relays[1].wait_recv()
            partner_sums(0)
            back[0].start()
            take_relay(2)
        if i == 9:
            for cp in spread:
                cp.wait_recv()
            l_m.wait()

            @pl.loop(0, 20)
            def _(k):
                rows = pl.ds(pl.multiple_of(k * 16, 16), 16)
                md = mean[rows, :]
                new_m = 0.9 * mo[rows, :] + md
                nm[rows, :] = new_m
                ng[rows, :] = gl[rows, :] - 0.7 * (0.9 * new_m + md)

            o_m = pltpu.make_async_copy(nm, nm_out, loc.at[5])
            o_g = pltpu.make_async_copy(ng, ng_out, loc.at[6])
            o_m.start()
            o_g.start()
        if i == 11:
            take_relay(3)
            relays[2].wait_recv()
            relays[3].wait_recv()
            partner_sums(1)
            back[1].start()

    def finish(core, g):
        rows = pl.ds(pl.multiple_of(core * 256 + g * 128, 128), 128)
        total = acc[rows, :] + PR[g, pl.ds(pl.multiple_of(core * 128, 128), 128), :].astype(F32)
        return (total * inv[rows, :][:, :1]).astype(BF16)

    swap = [
        remote(
            KS.at[pl.ds(g * 128, 128)], KO.at[pl.ds(g * 128, 128), own_cols], sib_s.at[2 + g], sib_r.at[2 + g], sib
        )
        for g in range(2)
    ]
    for g in range(2):
        back[g].wait_recv()
        KS[pl.ds(g * 128, 128), :] = finish(o, g)
        swap[g].start()
        KO[pl.ds(g * 128, 128), own_cols] = finish(c, g)
    for g in range(2):
        swap[g].wait_recv()
    o_k = pltpu.make_async_copy(KO, keys_out, loc.at[7])
    o_k.start()

    w_sib.wait_send()
    h_sib.wait_send()
    cross.wait_send()
    ysum.wait_send()
    for cp in [cp for grp in groups for cp in grp] + relays + ring[0] + ring[1] + back + scatter + spread + swap:
        cp.wait_send()
    o_m.wait()
    o_g.wait()
    o_k.wait()


def shards(hidden, norm_gain, local_weight, global_weight, momentum):
    weight_rows = local_weight[0]
    own = weight_rows.shape[0]
    gain = lax.dynamic_slice(norm_gain, (lax.axis_index("fsdp") * own,), (own,))
    scaled = (weight_rows.astype(F32) * gain[:, None]).astype(BF16)
    dma = pltpu.SemaphoreType.DMA
    V = pltpu.VMEM
    return tuple(pl.pallas_call(
        kernel,
        out_shape=(
            jax.ShapeDtypeStruct((256, 1024), BF16),
            jax.ShapeDtypeStruct((320, 1024), F32),
            jax.ShapeDtypeStruct((320, 1024), F32),
        ),
        in_specs=[pl.BlockSpec(memory_space=pl.ANY)] * 5,
        out_specs=(pl.BlockSpec(memory_space=pl.ANY),) * 3,
        scratch_shapes=[
            V((512, 10240), BF16), V((2, 256, 4096), BF16), V((8, 640, 512), BF16), V((8, 128, 512), BF16),
            V((512, 512), F32), V((2, 256, 512), BF16), V((2, 256, 512), BF16),
            V((320, 1024), BF16), V((320, 1024), F32), V((320, 1024), F32), V((320, 1024), F32),
            V((3, 80, 1024), F32), V((80, 1024), BF16), V((80, 1024), BF16), V((320, 1024), F32),
            V((320, 1024), F32), V((320, 1024), F32), V((512, 128), F32), V((256, 1024), BF16), V((256, 512), BF16),
            dma((8,)), dma((4,)), dma((4,)), dma((4,)), dma((4,)), dma((2, N_RING)), dma((2, N_RING)),
            dma, dma, dma((4, 4)), dma((4, 4)), dma((2,)), dma((2,)), dma((3,)), dma((3,)), dma((3,)), dma((3,)),
            dma, dma,
        ],
        compiler_params=pltpu.CompilerParams(
            collective_id=0, has_side_effects=True, vmem_limit_bytes=58 * 1024 * 1024
        ),
        cost_estimate=pl.CostEstimate(flops=5368709120, bytes_accessed=12000000, transcendentals=512),
    )(scaled, hidden, weight_rows, global_weight, momentum))


def solution(mesh):
    return jax.shard_map(
        shards,
        mesh=mesh,
        in_specs=(
            P(("replica", "fsdp"), None),
            P(),
            P("replica", "fsdp", None),
            P("fsdp", None),
            P("fsdp", None),
        ),
        out_specs=(P(("replica", "fsdp"), None), P("fsdp", None), P("fsdp", None)),
        check_vma=False,
    )
```

time: 263 us -> 98 us (0.37)
  waiting for transfers between devices: 192 us -> 0 us
  Pallas kernels: 0 us -> 88.6 us
  blocking collectives: 24 us -> 0 us
  matrix products: 14.4 us -> 0 us
  between operations: 14.1 us -> 0.65 us
  other arithmetic: 15.4 us -> 2.1 us
  local copies, waits for them, and re-layouts: 2.47 us -> 6.33 us
    all_gather x2 -> x0, waiting for transfers between devices: 191 us -> none  [the longest x1 151 us: shards(): lax.all_gather(weight_rows, 'fsdp', axis=0, tiled=True)]
    pallas_call x0 -> x1, Pallas kernels: none -> 88.6 us  [shards(): pl.pallas_call(kernel, out_shape=(jax.ShapeDtypeStruct((256, 1024), BF16)...]
    all_gather x1 -> x0, blocking collectives: 24 us -> none  [shards(): lax.all_gather(scale[None], 'replica', axis=0, tiled=True)]
    dot_general x1 -> x0, matrix products: 14.4 us -> none  [shards(): jnp.dot(normed, lax.all_gather(weight_rows, 'fsdp', axis=0, tiled=True),...]
    reduce_sum x2 -> x0, other arithmetic: 9.84 us -> none  [the longest x1 6.17 us: shards(): mean_delta = (jnp.sum(decoded, axis=0) / replicas).reshape(own_rows, width)]
    unnamed x9 -> x5, local copies, waits for them, and re-layouts: 2.21 us -> 5.56 us
  transfers between devices with their start and end apart: 2 -> 0, of which waited for: 2 -> 0; matrix products, arithmetic and copies ran while one was open for 5% -> 0% of each run, Pallas kernels for 0% -> 0%
where the time goes in v1:
time: 98 us; the launch traced here: 97.7 us
  Pallas kernels  88.6 us (90%)
  local copies, waits for them, and re-layouts  6.33 us (6%)
  other arithmetic  2.1 us (2%)
    pallas_call x1, Pallas kernels, shards(): pl.pallas_call(kernel, out_shape=(jax.ShapeDtypeStruct((256, 1024), BF16)...  88.6 us
    unnamed x5, local copies, waits for them, and re-layouts  5.56 us
    convert_element_type x1, other arithmetic, shards(): scaled = (weight_rows.astype(F32) * gain[:, None]).astype(BF16)  2.1 us

profile of v1, /device:TPU:1, one launch (start us, length us, event | category | flops | bytes accessed | tf_op | source)
XLA Modules:
  0.0 97.7 jit_solution(4354648412257723171)
XLA Ops:
  0.6 0.8 dynamic_slice.3
  1.4 2.1 %multiply_convert_fusion.ws = bf16[320,1024]{1,0:T(8,128)(2,1)} fusion(f32[320]{0:T(512)S(1)} %dynamic_slice.3, bf16[1,320,1024]{2,1,0:T(8,128)(2,1)} %param.7), kind=kLoop, calls=%fused_computation | loop fusion | flops 983040 | bytes 1312000 | tf_op jit(solution)/shard_map/convert_element_type | solution.py:325
  3.5 88.6 %shard_map.76 = (bf16[256,1024]{1,0:T(8,128)(2,1)}, f32[320,1024]{1,0:T(8,128)}, f32[320,1024]{1,0:T(8,128)}) custom-call(bf16[320,1024]{1,0:T(8,128)(2,1)} %multiply_convert_fusion.ws, bf16[256,10240]{1,0:T(8,128)(2,1)} %hid.1, bf16[320,1024]{1,0:T(8,128)(2,1)} %bitcast.2, f32[320,1024]{1,0:T(8,128)} %g_in.1, f32[320,1024]{1,0:T(8,128)} %m_in.1), custom_call_target="tpu_custom_call" | custom-call | flops 5368709120 | bytes 12000000 | tf_op jit(solution)/shard_map/pallas_call | solution.py:328
  92.2 1.9 %copy.11 = bf16[256,1024]{1,0:T(8,128)(2,1)} copy(bf16[256,1024]{1,0:T(8,128)(2,1)} %get-tuple-element.6) | data formatting | bytes 1048576
  94.0 0.0 copy-start
  94.0 2.6 %copy.12 = f32[320,1024]{1,0:T(8,128)} copy(f32[320,1024]{1,0:T(8,128)} %get-tuple-element.7) | data formatting | bytes 2621440
  96.7 0.0 copy-done
  96.7 1.1 %copy.13 = f32[320,1024]{1,0:T(8,128)} copy(f32[320,1024]{1,0:T(8,128)S(1)} %copy-done) | data formatting | bytes 2621440
Async XLA Ops:
  94.0 2.6 %copy-start = (f32[320,1024]{1,0:T(8,128)S(1)}, f32[320,1024]{1,0:T(8,128)}, u32[]{:S(2)}) copy-start(f32[320,1024]{1,0:T(8,128)} %get-tuple-element.8) | copy-start | bytes 3932164

commit v2 on v1

--- a/solution.py
+++ b/solution.py
@@ -18,11 +18,15 @@
     ("B", 1, 2), ("B", 0, 3), ("A", 0, 1), ("A", 1, 1), ("A", 0, 2), ("A", 1, 2), ("A", 0, 3),
 )
 N_RING = len(RING)
+RELAY_AT = (2, 4, 7, 9)
+SUM_AT = (8, 9)
+HID_FIRST = 3
+HID_NEXT = (2, 2, 2, 2, 1, 1, 2, 2, 0, 0, 0, 0, 0, 0)
 
 
 def kernel(
-    ws, hid, wl_in, g_in, m_in, keys_out, ng_out, nm_out,
-    H, HP, WB, WX, acc, PS, PR, wl, gl, mo, dec, rsb, ysend, yrecv, mean, ng, nm, inv, KO, KS,
+    gain_in, hid, wl_in, g_in, m_in, keys_out, ng_out, nm_out,
+    gain, SX, H, HP, WB, WX, acc, PS, PR, wl, gl, mo, dec, rsb, ysend, yrecv, mean, ng, nm, inv, KO, KS,
     loc, sib_s, sib_r, rel_s, rel_r, z_s, z_r, yc_s, yc_r, yh_s, yh_r, yp_s, yp_r, x_s, x_r, xg_s, xg_r, yl_s, yl_r,
 ):
     replica, fsdp = lax.axis_index("replica"), lax.axis_index("fsdp")
@@ -48,25 +52,39 @@
     own_cols = pl.ds(pl.multiple_of(c * 512, 512), 512)
     oth_cols = pl.ds(pl.multiple_of(o * 512, 512), 512)
     own_rows = pl.ds(pl.multiple_of(c * 320, 64), 320)
-    l_w = pltpu.make_async_copy(ws.at[:, own_cols], WB.at[z, own_rows], loc.at[1])
+    l_gain = pltpu.make_async_copy(gain_in, gain, loc.at[1])
     l_wl = pltpu.make_async_copy(wl_in, wl, loc.at[2])
     l_g = pltpu.make_async_copy(g_in, gl, loc.at[3])
     l_m = pltpu.make_async_copy(m_in, mo, loc.at[4])
-    l_w.start()
     l_wl.start()
-    l_g.start()
-    l_h.start()
-    l_m.start()
+    l_gain.start()
 
     barrier = pltpu.get_barrier_semaphore()
     everyone = [sib, zdev[0], zdev[1], partner, ydev] + xdev
     for dev in everyone:
         pl.semaphore_signal(barrier, inc=1, device_id=dev, device_id_type=MESH)
+
+    l_wl.wait()
+    l_gain.wait()
+
+    @pl.loop(0, 5)
+    def _(i):
+        rows = pl.ds(pl.multiple_of(i * 64, 64), 64)
+        unit = c * 5 + i
+        along = gain[pl.ds((r * 8 + z) * 5 + lax.div(unit, 2), 1), :]
+        lane = lax.broadcasted_iota(jnp.int32, (64, 128), 1)
+        row = lax.broadcasted_iota(jnp.int32, (64, 128), 0)
+        mine = lane - row == 64 * lax.rem(unit, 2)
+        column = jnp.sum(jnp.where(mine, jnp.broadcast_to(along, (64, 128)), 0.0), axis=-1, keepdims=True)
+        SX[rows, :] = (wl[rows, oth_cols].astype(F32) * column).astype(BF16)
+        WB[z, pl.ds(pl.multiple_of(c * 320 + i * 64, 64), 64), :] = (wl[rows, own_cols].astype(F32) * column).astype(BF16)
+
+    l_g.start()
+    l_h.start()
+    l_m.start()
     pl.semaphore_wait(barrier, len(everyone))
-
-    w_sib = remote(ws.at[:, oth_cols], WB.at[z, own_rows], sib_s.at[0], sib_r.at[0], sib)
+    w_sib = remote(SX, WB.at[z, own_rows], sib_s.at[0], sib_r.at[0], sib)
     w_sib.start()
-
     def hid_group(q):
         g, half = divmod(q, 2)
         out = []
@@ -86,6 +104,14 @@
 
     groups = [hid_group(q) for q in range(4)]
     relays = [relay(q) for q in range(4)]
+    queue = [cp for grp in groups for cp in grp]
+
+    def send_hidden(count):
+        for _ in range(min(count, len(queue))):
+            queue.pop(0).start()
+
+    send_hidden(HID_FIRST)
+
 
     def chunk_ref(kind, half, slot):
         if kind == "B":
@@ -104,23 +130,17 @@
 
     ring = [[ring_copy(way, i) for i in range(N_RING)] for way in range(2)]
 
-    l_w.wait()
     w_sib.wait_recv()
     for i in range(2):
         for way in range(2):
             ring[way][i].start()
     cross = remote(WB.at[z, pl.ds(512, 128)], WX.at[z], yc_s, yc_r, partner)
     cross.start()
-    for cp in groups[0]:
-        cp.start()
     h_sib = remote(
         hid, H.at[pl.ds(pl.multiple_of(c * 256, 256), 256)], sib_s.at[1], sib_r.at[1], sib
     )
     h_sib.start()
-    for cp in groups[1]:
-        cp.start()
-
-    l_wl.wait()
+
     l_g.wait()
 
     @pl.loop(0, 20)
@@ -181,8 +201,8 @@
 
     def mean_squares(part):
         @pl.loop(0, 4)
-        def _(i):
-            rows = pl.ds(pl.multiple_of(part * 256 + i * 64, 64), 64)
+        def _(k):
+            rows = pl.ds(pl.multiple_of(part * 256 + k * 64, 64), 64)
 
             def body(k, total):
                 for s in range(4):
@@ -212,9 +232,6 @@
         for cp in groups[q]:
             cp.wait_recv()
         relays[q].start()
-        if q + 2 < 4:
-            for cp in groups[q + 2]:
-                cp.start()
 
     for i in range(N_RING):
         for way in range(2):
@@ -223,10 +240,12 @@
                 if i == 2 and way == 0:
                     cross.wait_recv()
                 ring[way][i + 2].start()
+        send_hidden(HID_NEXT[i])
+        for q in range(4):
+            if RELAY_AT[q] == i:
+                take_relay(q)
         if i == 2:
-            l_h.wait()
             h_sib.wait_recv()
-            take_relay(0)
             for half in range(2):
                 mm_chunk("B", half, z)
                 mm_chunk("A", half, z)
@@ -241,10 +260,11 @@
             ysum.start()
         elif i > 2:
             mm_arrival(i)
+        if i == 0:
+            l_h.wait()
+            mean_squares(c)
         if i == 3:
-            mean_squares(0)
-        if i == 4:
-            mean_squares(1)
+            mean_squares(o)
         if i == 5:
             ysum.wait_recv()
             for k in range(5):
@@ -254,14 +274,11 @@
                 ) * 0.125
             for cp in spread:
                 cp.start()
-        if i == 6:
-            take_relay(1)
-        if i == 8:
+        if i == SUM_AT[0]:
             relays[0].wait_recv()
             relays[1].wait_recv()
             partner_sums(0)
             back[0].start()
-            take_relay(2)
         if i == 9:
             for cp in spread:
                 cp.wait_recv()
@@ -279,8 +296,7 @@
             o_g = pltpu.make_async_copy(ng, ng_out, loc.at[6])
             o_m.start()
             o_g.start()
-        if i == 11:
-            take_relay(3)
+        if i == SUM_AT[1]:
             relays[2].wait_recv()
             relays[3].wait_recv()
             partner_sums(1)
@@ -320,9 +336,6 @@
 
 def shards(hidden, norm_gain, local_weight, global_weight, momentum):
     weight_rows = local_weight[0]
-    own = weight_rows.shape[0]
-    gain = lax.dynamic_slice(norm_gain, (lax.axis_index("fsdp") * own,), (own,))
-    scaled = (weight_rows.astype(F32) * gain[:, None]).astype(BF16)
     dma = pltpu.SemaphoreType.DMA
     V = pltpu.VMEM
     return tuple(pl.pallas_call(
@@ -335,7 +348,7 @@
         in_specs=[pl.BlockSpec(memory_space=pl.ANY)] * 5,
         out_specs=(pl.BlockSpec(memory_space=pl.ANY),) * 3,
         scratch_shapes=[
-            V((512, 10240), BF16), V((2, 256, 4096), BF16), V((8, 640, 512), BF16), V((8, 128, 512), BF16),
+            V((80, 128), F32), V((320, 512), BF16), V((512, 10240), BF16), V((2, 256, 4096), BF16), V((8, 640, 512), BF16), V((8, 128, 512), BF16),
             V((512, 512), F32), V((2, 256, 512), BF16), V((2, 256, 512), BF16),
             V((320, 1024), BF16), V((320, 1024), F32), V((320, 1024), F32), V((320, 1024), F32),
             V((3, 80, 1024), F32), V((80, 1024), BF16), V((80, 1024), BF16), V((320, 1024), F32),
@@ -345,10 +358,10 @@
             dma, dma,
         ],
         compiler_params=pltpu.CompilerParams(
-            collective_id=0, has_side_effects=True, vmem_limit_bytes=58 * 1024 * 1024
+            collective_id=0, has_side_effects=True, vmem_limit_bytes=50 * 1024 * 1024
         ),
         cost_estimate=pl.CostEstimate(flops=5368709120, bytes_accessed=12000000, transcendentals=512),
-    )(scaled, hidden, weight_rows, global_weight, momentum))
+    )(norm_gain.reshape(80, 128), hidden, weight_rows, global_weight, momentum))
 
 
 def solution(mesh):

time: 98 us -> 86.1 us (0.88)
  Pallas kernels: 88.6 us -> 80.5 us
  other arithmetic: 2.1 us -> 0 us
  local copies, waits for them, and re-layouts: 6.33 us -> 4.77 us
    pallas_call x1, Pallas kernels: 88.6 us -> 80.5 us  [shards(): pl.pallas_call(kernel, out_shape=(jax.ShapeDtypeStruct((256, 1024), BF16)...]
    convert_element_type x1 -> x0, other arithmetic: 2.1 us -> none  [shards(): scaled = (weight_rows.astype(F32) * gain[:, None]).astype(BF16)]
    unnamed x5 -> x7, local copies, waits for them, and re-layouts: 5.56 us -> 4.77 us
where the time goes in v2:
time: 86.1 us; the launch traced here: 85.9 us
  Pallas kernels  80.5 us (93%)
  local copies, waits for them, and re-layouts  4.77 us (6%)
    pallas_call x1, Pallas kernels, shards(): pl.pallas_call(kernel, out_shape=(jax.ShapeDtypeStruct((256, 1024), BF16)...  80.5 us
    unnamed x7, local copies, waits for them, and re-layouts  4.77 us

profile of v2, /device:TPU:1, one launch (start us, length us, event | category | flops | bytes accessed | tf_op | source)
XLA Modules:
  0.0 85.9 jit_solution(4570209456149205166)
XLA Ops:
  0.6 0.0 copy-start
  0.6 1.1 %copy-done = bf16[1,320,1024]{2,1,0:T(8,128)(2,1)S(1)} copy-done((bf16[1,320,1024]{2,1,0:T(8,128)(2,1)S(1)}, bf16[1,320,1024]{2,1,0:T(8,128)(2,1)}, u32[]{:S(2)}) %copy-start) | copy-done | bytes 655384
  1.7 0.0 copy-start.1
  1.7 0.8 copy-done.1
  2.5 80.5 %shard_map.76 = (bf16[256,1024]{1,0:T(8,128)(2,1)S(1)}, f32[320,1024]{1,0:T(8,128)S(1)}, f32[320,1024]{1,0:T(8,128)S(1)}) custom-call(f32[80,128]{1,0:T(8,128)S(1)} %bitcast.3, bf16[256,10240]{1,0:T(8,128)(2,1)} %hid.1, bf16[320,1024]{1,0:T(8,128)(2,1)S(1)} %bitcast.2, f32[320,1024]{1,0:T(8,128)} %g_in.1, f32[320,1024]{1,0:T(8,128)} %m_in.1), custom_call_target="tpu_custom_call" | custom-call | flops 5368709120 | bytes 12000000 | tf_op jit(solution)/shard_map/pallas_call | solution.py:341
  83.0 0.8 copy.11
  83.8 1.1 %copy.12 = f32[320,1024]{1,0:T(8,128)} copy(f32[320,1024]{1,0:T(8,128)S(1)} %get-tuple-element.7) | data formatting | bytes 2621440
  84.8 1.1 %copy.13 = f32[320,1024]{1,0:T(8,128)} copy(f32[320,1024]{1,0:T(8,128)S(1)} %get-tuple-element.8) | data formatting | bytes 2621440
Async XLA Ops:
  0.6 1.1 %copy-start = (bf16[1,320,1024]{2,1,0:T(8,128)(2,1)S(1)}, bf16[1,320,1024]{2,1,0:T(8,128)(2,1)}, u32[]{:S(2)}) copy-start(bf16[1,320,1024]{2,1,0:T(8,128)(2,1)} %param.7) | copy-start | bytes 1966084
  1.7 0.8 copy-start.1

commit v3 on v2

--- a/solution.py
+++ b/solution.py
@@ -18,15 +18,16 @@
     ("B", 1, 2), ("B", 0, 3), ("A", 0, 1), ("A", 1, 1), ("A", 0, 2), ("A", 1, 2), ("A", 0, 3),
 )
 N_RING = len(RING)
-RELAY_AT = (2, 4, 7, 9)
-SUM_AT = (8, 9)
+RELAY_AT = (2, 4, 7, 10)
+SUM_AT = (8, 10)
+STATE_AT = 11
 HID_FIRST = 3
 HID_NEXT = (2, 2, 2, 2, 1, 1, 2, 2, 0, 0, 0, 0, 0, 0)
 
 
 def kernel(
     gain_in, hid, wl_in, g_in, m_in, keys_out, ng_out, nm_out,
-    gain, SX, H, HP, WB, WX, acc, PS, PR, wl, gl, mo, dec, rsb, ysend, yrecv, mean, ng, nm, inv, KO, KS,
+    gain, SX, H, HP, WB, WX, acc, accp, PS, PR, wl, gl, mo, dec, rsb, ysend, yrecv, mean, ng, nm, inv, KO, KS,
     loc, sib_s, sib_r, rel_s, rel_r, z_s, z_r, yc_s, yc_r, yh_s, yh_r, yp_s, yp_r, x_s, x_r, xg_s, xg_r, yl_s, yl_r,
 ):
     replica, fsdp = lax.axis_index("replica"), lax.axis_index("fsdp")
@@ -214,19 +215,30 @@
             ms = jnp.sum(total, axis=-1, keepdims=True) * (1.0 / 10240)
             inv[rows, :] = jnp.broadcast_to(lax.rsqrt(ms + 1e-05) * (1.0 / math.sqrt(10240)), (64, 128))
 
-    def partner_sums(g):
+    def partner_mm(g, slot, first=False):
+        left = HP[g, :, pl.ds(pl.multiple_of(slot * 512, 512), 512)]
         for n in range(2):
             cols = pl.ds(n * 256, 256)
-
-            def body(s, total):
-                return total + jnp.dot(
-                    HP[g, :, pl.ds(pl.multiple_of(s * 512, 512), 512)],
-                    WB[s, pl.ds(0, 512), cols], preferred_element_type=F32,
-                )
-
-            PS[g, :, cols] = lax.fori_loop(0, 8, body, jnp.zeros((256, 256), F32)).astype(BF16)
-
-    back = [remote(PS.at[g], PR.at[g], yp_s.at[g], yp_r.at[g], partner) for g in range(2)]
+            part = jnp.dot(left, WB[slot, pl.ds(0, 512), cols], preferred_element_type=F32)
+            accp[:, cols] = part if first else accp[:, cols] + part
+
+    back = [
+        [
+            remote(
+                PS.at[g, pl.ds(pl.multiple_of(core * 128, 128), 128)],
+                PR.at[g, pl.ds(pl.multiple_of(core * 128, 128), 128)],
+                yp_s.at[g, k], yp_r.at[g, k], partner,
+            )
+            for k, core in enumerate((o, c))
+        ]
+        for g in range(2)
+    ]
+
+    def send_back(g):
+        PS[g] = accp[...].astype(BF16)
+        for cp in back[g]:
+            cp.start()
+
 
     def take_relay(q):
         for cp in groups[q]:
@@ -274,12 +286,31 @@
                 ) * 0.125
             for cp in spread:
                 cp.start()
-        if i == SUM_AT[0]:
+        if i == SUM_AT[0] - 2:
             relays[0].wait_recv()
             relays[1].wait_recv()
-            partner_sums(0)
-            back[0].start()
-        if i == 9:
+            partner_mm(0, z, first=True)
+
+            @pl.loop(0, 4)
+            def _(k):
+                partner_mm(0, lax.rem(z + jnp.where(k < 2, k + 1, k + 4), 8))
+
+        if i == SUM_AT[0] - 1:
+            @pl.loop(0, 2)
+            def _(k):
+                partner_mm(0, lax.rem(z + 3 + 2 * k, 8))
+
+        if i == SUM_AT[0]:
+            partner_mm(0, lax.rem(z + 4, 8))
+            send_back(0)
+            relays[2].wait_recv()
+            partner_mm(1, 0, first=True)
+
+            @pl.loop(1, 4)
+            def _(k):
+                partner_mm(1, k)
+
+        if i == STATE_AT:
             for cp in spread:
                 cp.wait_recv()
             l_m.wait()
@@ -297,10 +328,13 @@
             o_m.start()
             o_g.start()
         if i == SUM_AT[1]:
-            relays[2].wait_recv()
             relays[3].wait_recv()
-            partner_sums(1)
-            back[1].start()
+
+            @pl.loop(4, 8)
+            def _(k):
+                partner_mm(1, k)
+
+            send_back(1)
 
     def finish(core, g):
         rows = pl.ds(pl.multiple_of(core * 256 + g * 128, 128), 128)
@@ -314,9 +348,10 @@
         for g in range(2)
     ]
     for g in range(2):
-        back[g].wait_recv()
+        back[g][0].wait_recv()
         KS[pl.ds(g * 128, 128), :] = finish(o, g)
         swap[g].start()
+        back[g][1].wait_recv()
         KO[pl.ds(g * 128, 128), own_cols] = finish(c, g)
     for g in range(2):
         swap[g].wait_recv()
@@ -327,18 +362,29 @@
     h_sib.wait_send()
     cross.wait_send()
     ysum.wait_send()
-    for cp in [cp for grp in groups for cp in grp] + relays + ring[0] + ring[1] + back + scatter + spread + swap:
+    for cp in [cp for grp in groups for cp in grp] + relays + ring[0] + ring[1] + back[0] + back[1] + scatter + spread + swap:
         cp.wait_send()
     o_m.wait()
     o_g.wait()
     o_k.wait()
 
 
+def write_out(a, b, c, a_out, b_out, c_out, sems):
+    copies = [
+        pltpu.make_async_copy(src, dst, sems.at[i])
+        for i, (src, dst) in enumerate(((a, a_out), (b, b_out), (c, c_out)))
+    ]
+    for cp in copies:
+        cp.start()
+    for cp in copies:
+        cp.wait()
+
+
 def shards(hidden, norm_gain, local_weight, global_weight, momentum):
     weight_rows = local_weight[0]
     dma = pltpu.SemaphoreType.DMA
     V = pltpu.VMEM
-    return tuple(pl.pallas_call(
+    parts = tuple(pl.pallas_call(
         kernel,
         out_shape=(
             jax.ShapeDtypeStruct((256, 1024), BF16),
@@ -349,19 +395,27 @@
         out_specs=(pl.BlockSpec(memory_space=pl.ANY),) * 3,
         scratch_shapes=[
             V((80, 128), F32), V((320, 512), BF16), V((512, 10240), BF16), V((2, 256, 4096), BF16), V((8, 640, 512), BF16), V((8, 128, 512), BF16),
-            V((512, 512), F32), V((2, 256, 512), BF16), V((2, 256, 512), BF16),
+            V((512, 512), F32), V((256, 512), F32), V((2, 256, 512), BF16), V((2, 256, 512), BF16),
             V((320, 1024), BF16), V((320, 1024), F32), V((320, 1024), F32), V((320, 1024), F32),
             V((3, 80, 1024), F32), V((80, 1024), BF16), V((80, 1024), BF16), V((320, 1024), F32),
             V((320, 1024), F32), V((320, 1024), F32), V((512, 128), F32), V((256, 1024), BF16), V((256, 512), BF16),
             dma((8,)), dma((4,)), dma((4,)), dma((4,)), dma((4,)), dma((2, N_RING)), dma((2, N_RING)),
-            dma, dma, dma((4, 4)), dma((4, 4)), dma((2,)), dma((2,)), dma((3,)), dma((3,)), dma((3,)), dma((3,)),
+            dma, dma, dma((4, 4)), dma((4, 4)), dma((2, 2)), dma((2, 2)), dma((3,)), dma((3,)), dma((3,)), dma((3,)),
             dma, dma,
         ],
         compiler_params=pltpu.CompilerParams(
             collective_id=0, has_side_effects=True, vmem_limit_bytes=50 * 1024 * 1024
         ),
         cost_estimate=pl.CostEstimate(flops=5368709120, bytes_accessed=12000000, transcendentals=512),
-    )(norm_gain.reshape(80, 128), hidden, weight_rows, global_weight, momentum))
+    )(pltpu.with_memory_space_constraint(norm_gain.reshape(80, 128), pltpu.HBM), hidden, pltpu.with_memory_space_constraint(weight_rows, pltpu.HBM), global_weight, momentum))
+    return tuple(pl.pallas_call(
+        write_out,
+        out_shape=tuple(jax.ShapeDtypeStruct(part.shape, part.dtype) for part in parts),
+        in_specs=[pl.BlockSpec(memory_space=pltpu.VMEM)] * 3,
+        out_specs=(pl.BlockSpec(memory_space=pl.ANY),) * 3,
+        scratch_shapes=[dma((3,))],
+        compiler_params=pltpu.CompilerParams(vmem_limit_bytes=8 * 1024 * 1024),
+    )(*parts))
 
 
 def solution(mesh):

time: 86.1 us -> 78.8 us (0.915)
  local copies, waits for them, and re-layouts: 4.77 us -> 0 us
  Pallas kernels: 80.5 us -> 78 us
    unnamed x7 -> x0, local copies, waits for them, and re-layouts: 4.77 us -> none
    pallas_call x1, Pallas kernels: 80.5 us -> 76.3 us  [shards(): pl.pallas_call(kernel, out_shape=(jax.ShapeDtypeStruct((256, 1024), BF16)...]
    pallas_call x0 -> x1, Pallas kernels: none -> 1.69 us  [shards(): pl.pallas_call(write_out, out_shape=tuple((jax.ShapeDtypeStruct(part.shap...]
where the time goes in v3:
time: 78.8 us; the launch traced here: 78.7 us
  Pallas kernels  78 us (99%)
    pallas_call x1, Pallas kernels, shards(): pl.pallas_call(kernel, out_shape=(jax.ShapeDtypeStruct((256, 1024), BF16)...  76.3 us
    pallas_call x1, Pallas kernels, shards(): pl.pallas_call(write_out, out_shape=tuple((jax.ShapeDtypeStruct(part.shap...  1.69 us

profile of v3, /device:TPU:1, one launch (start us, length us, event | category | flops | bytes accessed | tf_op | source)
XLA Modules:
  0.0 78.7 jit_solution(15369519491184375457)
XLA Ops:
  0.6 76.3 %shard_map.76 = (bf16[256,1024]{1,0:T(8,128)(2,1)S(1)}, f32[320,1024]{1,0:T(8,128)S(1)}, f32[320,1024]{1,0:T(8,128)S(1)}) custom-call(f32[80,128]{1,0:T(8,128)} %bitcast.3, bf16[256,10240]{1,0:T(8,128)(2,1)} %hid.1, bf16[320,1024]{1,0:T(8,128)(2,1)} %bitcast.2, f32[320,1024]{1,0:T(8,128)} %g_in.1, f32[320,1024]{1,0:T(8,128)} %m_in.1), custom_call_target="tpu_custom_call" | custom-call | flops 5368709120 | bytes 12000000 | tf_op jit(solution)/shard_map/pallas_call | solution.py:387
  77.0 1.7 %shard_map.77 = (bf16[256,1024]{1,0:T(8,128)(2,1)}, f32[320,1024]{1,0:T(8,128)}, f32[320,1024]{1,0:T(8,128)}) custom-call(bf16[256,1024]{1,0:T(8,128)(2,1)S(1)} %get-tuple-element.6.a, f32[320,1024]{1,0:T(8,128)S(1)} %get-tuple-element.7.b, f32[320,1024]{1,0:T(8,128)S(1)} %get-tuple-element.8.c), custom_call_target="tpu_custom_call" | custom-call | tf_op jit(solution)/shard_map/pallas_call | solution.py:411

commit v4 on v3

--- a/solution.py
+++ b/solution.py
@@ -28,7 +28,7 @@
 def kernel(
     gain_in, hid, wl_in, g_in, m_in, keys_out, ng_out, nm_out,
     gain, SX, H, HP, WB, WX, acc, accp, PS, PR, wl, gl, mo, dec, rsb, ysend, yrecv, mean, ng, nm, inv, KO, KS,
-    loc, sib_s, sib_r, rel_s, rel_r, z_s, z_r, yc_s, yc_r, yh_s, yh_r, yp_s, yp_r, x_s, x_r, xg_s, xg_r, yl_s, yl_r,
+    loc, hs_s, hs_r, sib_s, sib_r, rel_s, rel_r, z_s, z_r, yc_s, yc_r, yh_s, yh_r, yp_s, yp_r, x_s, x_r, xg_s, xg_r, yl_s, yl_r,
 ):
     replica, fsdp = lax.axis_index("replica"), lax.axis_index("fsdp")
     x, ylo = lax.rem(replica, 4), lax.div(replica, 4)
@@ -137,10 +137,15 @@
             ring[way][i].start()
     cross = remote(WB.at[z, pl.ds(512, 128)], WX.at[z], yc_s, yc_r, partner)
     cross.start()
-    h_sib = remote(
-        hid, H.at[pl.ds(pl.multiple_of(c * 256, 256), 256)], sib_s.at[1], sib_r.at[1], sib
-    )
-    h_sib.start()
+    h_sib = [
+        remote(
+            hid.at[pl.ds(k * 64, 64)], H.at[pl.ds(pl.multiple_of(c * 256 + k * 64, 64), 64)],
+            hs_s.at[k], hs_r.at[k], sib,
+        )
+        for k in range(4)
+    ]
+    h_sib[0].start()
+    h_sib[1].start()
 
     l_g.wait()
 
@@ -257,7 +262,8 @@
             if RELAY_AT[q] == i:
                 take_relay(q)
         if i == 2:
-            h_sib.wait_recv()
+            for cp in h_sib:
+                cp.wait_recv()
             for half in range(2):
                 mm_chunk("B", half, z)
                 mm_chunk("A", half, z)
@@ -273,6 +279,8 @@
         elif i > 2:
             mm_arrival(i)
         if i == 0:
+            h_sib[2].start()
+            h_sib[3].start()
             l_h.wait()
             mean_squares(c)
         if i == 3:
@@ -341,9 +349,15 @@
         total = acc[rows, :] + PR[g, pl.ds(pl.multiple_of(core * 128, 128), 128), :].astype(F32)
         return (total * inv[rows, :][:, :1]).astype(BF16)
 
+    o_k = [
+        pltpu.make_async_copy(
+            KO.at[pl.ds(g * 128, 128)], keys_out.at[pl.ds(g * 128, 128), own_cols], loc.at[7 + g]
+        )
+        for g in range(2)
+    ]
     swap = [
         remote(
-            KS.at[pl.ds(g * 128, 128)], KO.at[pl.ds(g * 128, 128), own_cols], sib_s.at[2 + g], sib_r.at[2 + g], sib
+            KS.at[pl.ds(g * 128, 128)], keys_out.at[pl.ds(g * 128, 128), own_cols], sib_s.at[2 + g], sib_r.at[2 + g], sib
         )
         for g in range(2)
     ]
@@ -352,21 +366,22 @@
         KS[pl.ds(g * 128, 128), :] = finish(o, g)
         swap[g].start()
         back[g][1].wait_recv()
-        KO[pl.ds(g * 128, 128), own_cols] = finish(c, g)
+        KO[pl.ds(g * 128, 128), :] = finish(c, g)
+        o_k[g].start()
     for g in range(2):
         swap[g].wait_recv()
-    o_k = pltpu.make_async_copy(KO, keys_out, loc.at[7])
-    o_k.start()
 
     w_sib.wait_send()
-    h_sib.wait_send()
+    for cp in h_sib:
+        cp.wait_send()
     cross.wait_send()
     ysum.wait_send()
     for cp in [cp for grp in groups for cp in grp] + relays + ring[0] + ring[1] + back[0] + back[1] + scatter + spread + swap:
         cp.wait_send()
     o_m.wait()
     o_g.wait()
-    o_k.wait()
+    o_k[0].wait()
+    o_k[1].wait()
 
 
 def write_out(a, b, c, a_out, b_out, c_out, sems):
@@ -398,8 +413,8 @@
             V((512, 512), F32), V((256, 512), F32), V((2, 256, 512), BF16), V((2, 256, 512), BF16),
             V((320, 1024), BF16), V((320, 1024), F32), V((320, 1024), F32), V((320, 1024), F32),
             V((3, 80, 1024), F32), V((80, 1024), BF16), V((80, 1024), BF16), V((320, 1024), F32),
-            V((320, 1024), F32), V((320, 1024), F32), V((512, 128), F32), V((256, 1024), BF16), V((256, 512), BF16),
-            dma((8,)), dma((4,)), dma((4,)), dma((4,)), dma((4,)), dma((2, N_RING)), dma((2, N_RING)),
+            V((320, 1024), F32), V((320, 1024), F32), V((512, 128), F32), V((256, 512), BF16), V((256, 512), BF16),
+            dma((9,)), dma((4,)), dma((4,)), dma((4,)), dma((4,)), dma((4,)), dma((4,)), dma((2, N_RING)), dma((2, N_RING)),
             dma, dma, dma((4, 4)), dma((4, 4)), dma((2, 2)), dma((2, 2)), dma((3,)), dma((3,)), dma((3,)), dma((3,)),
             dma, dma,
         ],

time: 78.8 us -> 78.8 us (level)
  no operation moved by 1% of the time
where the time goes in v4:
time: 78.8 us; the launch traced here: 78.7 us
  Pallas kernels  78.1 us (99%)
    pallas_call x1, Pallas kernels, shards(): pl.pallas_call(kernel, out_shape=(jax.ShapeDtypeStruct((256, 1024), BF16)...  76.4 us
    pallas_call x1, Pallas kernels, shards(): pl.pallas_call(write_out, out_shape=tuple((jax.ShapeDtypeStruct(part.shap...  1.69 us

profile of v4, /device:TPU:1, one launch (start us, length us, event | category | flops | bytes accessed | tf_op | source)
XLA Modules:
  0.0 78.7 jit_solution(572865493578045194)
XLA Ops:
  0.6 76.4 %shard_map.76 = (bf16[256,1024]{1,0:T(8,128)(2,1)S(1)}, f32[320,1024]{1,0:T(8,128)S(1)}, f32[320,1024]{1,0:T(8,128)S(1)}) custom-call(f32[80,128]{1,0:T(8,128)} %bitcast.3, bf16[256,10240]{1,0:T(8,128)(2,1)} %hid.1, bf16[320,1024]{1,0:T(8,128)(2,1)} %bitcast.2, f32[320,1024]{1,0:T(8,128)} %g_in.1, f32[320,1024]{1,0:T(8,128)} %m_in.1), custom_call_target="tpu_custom_call" | custom-call | flops 5368709120 | bytes 12000000 | tf_op jit(solution)/shard_map/pallas_call | solution.py:402
  77.1 1.7 %shard_map.77 = (bf16[256,1024]{1,0:T(8,128)(2,1)}, f32[320,1024]{1,0:T(8,128)}, f32[320,1024]{1,0:T(8,128)}) custom-call(bf16[256,1024]{1,0:T(8,128)(2,1)S(1)} %get-tuple-element.6.a, f32[320,1024]{1,0:T(8,128)S(1)} %get-tuple-element.7.b, f32[320,1024]{1,0:T(8,128)S(1)} %get-tuple-element.8.c), custom_call_target="tpu_custom_call" | custom-call | tf_op jit(solution)/shard_map/pallas_call | solution.py:426
